TPU v7x, 32 devices: a whole 2x2x4 slice. The times are simulated.
32 devices in a mesh: grp: 2 (over x), req: 16 (over z, y, core).
Axes of the slice: x: 2, y: 2, z: 4, core: 2. Of those that a mesh axis runs over, the one named last changes fastest.
Arguments:
- xbc: bfloat16 [4096, 9216], P(('grp', 'req')), parts along dimension 0, may hold values from -6 to 6
- dt_raw: float32 [4096, 128], P(('grp', 'req')), parts along dimension 0, may hold values from -6 to 6
- conv_weight: float32 [4, 9216], replicated, may hold values from -3 to 3
- conv_bias: float32 [9216], replicated, may hold values from -3 to 3
- dt_bias: float32 [128], replicated, may hold values from -1 to 1
- a_log: float32 [128], replicated, may hold values from -6 to -2.5
- d_skip: float32 [128], replicated, may hold values from 0.5 to 1.5
- cache_states: bfloat16 [96, 128, 8192], P(('grp', 'req')), parts along dimension 0, may hold values from -24 to 24
- cache_tails: bfloat16 [96, 3, 9216], P(('grp', 'req')), parts along dimension 0, may hold values from -6 to 6
- hit_owner: int32 [32], P('grp'), parts along dimension 0, may hold values from 0 to 15, as said below
- hit_slot: int32 [32], P('grp'), parts along dimension 0, may hold values from 0 to 2, as said below
- hit_spans: int32 [32], P('grp'), parts along dimension 0, may hold values from 0 to 4
- request_of: int32 [32], P(('grp', 'req')), parts along dimension 0, may hold values from 0 to 15, each once
Outputs:
- y_out: bfloat16 [4096, 8192], P(('grp', 'req')), parts along dimension 0
- final_state: bfloat16 [32, 128, 8192], P(('grp', 'req')), parts along dimension 0
There are 2 independent parts, one for each index of `grp`. A program takes and returns all parts, laid end to end along the dimension named above; an argument that names none is the same for every part. Nothing has to cross between parts.
Inputs may be any that keep to these rules, and one draw needn't show every extreme that they name: `hit_owner`: owners are skewed: some devices hold the prefixes of several requests, others of none. `hit_slot`: all requests that name the same owner device name the same slot of it. `request_of`: each request stands on exactly one device.
All inputs are finite; a program needn't handle non-finite values.
Results may differ from a plain program's by a relative error of at most 0.0039.
Values may be sent and summed in bfloat16 or wider, within the bound.
A program may use at most 128 MiB of HBM per device.

v0:
```python
import jax
import jax.numpy as jnp
from jax import lax
from jax.sharding import PartitionSpec as P

HEADS = 128
HEAD_DIM = 64
GROUPS = 4
NST = 128
INNER = 8192


def convolve(xrows, tail, conv_weight, conv_bias):
    rows = xrows.shape[0]
    taps = conv_weight.shape[0]
    extended = jnp.concatenate([tail, xrows], axis=0).astype(jnp.float32)
    conv = jnp.zeros((rows, xrows.shape[1]), jnp.float32) + conv_bias[None, :]
    for k in range(taps):
        conv = conv + conv_weight[k][None, :] * extended[k : k + rows]
    return jax.nn.silu(conv).astype(jnp.bfloat16)


def local_part(conv_out, dt_rows, dt_bias, a_log, d_skip):
    rows = conv_out.shape[0]
    per_group = HEADS // GROUPS
    inputs = conv_out[:, :INNER].reshape(rows, GROUPS, per_group, HEAD_DIM)
    b_part = conv_out[:, INNER : INNER + GROUPS * NST].reshape(rows, GROUPS, NST)
    c_part = conv_out[:, INNER + GROUPS * NST :].reshape(rows, GROUPS, NST)
    step = jax.nn.softplus(dt_rows + dt_bias[None, :])
    cum = jnp.cumsum(step * (-jnp.exp(a_log))[None, :], axis=0)
    scores = jnp.einsum("tgn,sgn->gts", c_part, b_part, preferred_element_type=jnp.float32)
    diff = cum.T[:, :, None] - cum.T[:, None, :]
    causal = lax.broadcasted_iota(jnp.int32, (rows, rows), 0) >= lax.broadcasted_iota(
        jnp.int32, (rows, rows), 1
    )
    decay = jnp.where(causal[None], jnp.exp(jnp.minimum(diff, 0.0)), 0.0)
    mixing = (
        scores[:, None]
        * decay.reshape(GROUPS, per_group, rows, rows)
        * step.T.reshape(GROUPS, per_group, 1, rows)
    ).astype(jnp.bfloat16)
    y_intra = jnp.einsum("gjts,sgjp->tgjp", mixing, inputs, preferred_element_type=jnp.float32)
    y_local = y_intra + d_skip.reshape(1, GROUPS, per_group, 1) * inputs.astype(jnp.float32)
    last = cum[rows - 1]
    carried = (
        (jnp.exp(last[None, :] - cum) * step).reshape(rows, GROUPS, per_group, 1)
        * inputs.astype(jnp.float32)
    ).astype(jnp.bfloat16)
    fresh = jnp.einsum("sgn,sgjp->ngjp", b_part, carried, preferred_element_type=jnp.float32)
    return (y_local, fresh, c_part, cum)


def state_part(start, c_part, cum):
    rows = c_part.shape[0]
    per_group = HEADS // GROUPS
    start_view = start.reshape(NST, GROUPS, per_group, HEAD_DIM)
    y_state = jnp.einsum("tgn,ngjp->tgjp", c_part, start_view, preferred_element_type=jnp.float32)
    y_state = y_state * jnp.exp(cum).reshape(rows, GROUPS, per_group, 1)
    kept = jnp.exp(cum[rows - 1]).reshape(1, GROUPS, per_group, 1) * start_view.astype(jnp.float32)
    return (y_state, kept)


def local(
    xbc,
    dt_raw,
    conv_weight,
    conv_bias,
    dt_bias,
    a_log,
    d_skip,
    cache_states,
    cache_tails,
    hit_owner,
    hit_slot,
    hit_spans,
    request_of,
):
    slots = cache_states.shape[0]
    every_request = lax.all_gather(request_of, "req", axis=0, tiled=True)
    mine = request_of[0]
    own_row = hit_owner[mine] * slots + hit_slot[mine]
    live = hit_spans[mine] > 0
    device = lax.axis_index("req")
    served = jnp.max(jnp.where(hit_owner == device, hit_slot, 0))
    send_states = lax.dynamic_slice_in_dim(cache_states, served, 1, 0)
    wanted_rows = hit_owner[every_request]
    every_tail = lax.all_gather(cache_tails, "req", axis=0, tiled=True)
    tail = lax.dynamic_index_in_dim(every_tail, own_row, 0, keepdims=False)
    state_parts = lax.all_to_all(send_states, "req", split_axis=2, concat_axis=0, tiled=True)
    state_chosen = jnp.take(state_parts, wanted_rows, axis=0)
    start = lax.all_to_all(state_chosen, "req", split_axis=0, concat_axis=2, tiled=True)[0]
    tail = jnp.where(live, tail, jnp.zeros_like(tail))
    start = jnp.where(live, start, jnp.zeros_like(start))
    conv_out = convolve(xbc, tail, conv_weight, conv_bias)
    y_local, fresh, c_part, cum = local_part(conv_out, dt_raw, dt_bias, a_log, d_skip)
    y_state, kept = state_part(start, c_part, cum)
    rows = xbc.shape[0]
    y_out = (y_local + y_state).reshape(rows, INNER).astype(jnp.bfloat16)
    final_state = (kept + fresh).reshape(1, NST, INNER).astype(jnp.bfloat16)
    return (y_out, final_state)


def solution(mesh):
    in_specs = (
        P(("grp", "req"), None),
        P(("grp", "req"), None),
        P(),
        P(),
        P(),
        P(),
        P(),
        P(("grp", "req"), None, None),
        P(("grp", "req"), None, None),
        P("grp"),
        P("grp"),
        P("grp"),
        P(("grp", "req")),
    )
    out_specs = (P(("grp", "req"), None), P(("grp", "req"), None, None))
    return jax.shard_map(local, mesh=mesh, in_specs=in_specs, out_specs=out_specs, check_vma=False)
```

profile of v0, /device:TPU:15, one launch (start us, length us, event | category | flops | bytes accessed | tf_op | source)
XLA Modules:
  0.0 240.6 jit_solution(13793065196203515922)
XLA Ops:
  9.9 7.9 %all-reduce = s32[16]{0:T(128)S(1)} all-reduce(s32[16]{0:T(128)S(1)} %dynamic-update-slice), channel_id=1, replica_groups=mesh['grp'=2,'req'=16] {'req'}, use_global_device_ids=true, to_apply=%add | all-reduce | flops 16 | bytes 128
  21.1 1.7 constant_dynamic-slice_fusion
  22.8 6.9 %copy.73 = bf16[1,128,8192]{1,0,2:T(2,128)(2,1)} copy(bf16[1,128,8192]{2,1,0:T(8,128)(2,1)S(1)} %constant_dynamic-slice_fusion) | data formatting | bytes 4194304
  30.2 45.2 %reduce.4 = bf16[8192,128]{1,0:T(8,128)(2,1)S(1)} reduce(bf16[8192,1,128]{2,1,0:T(2,128)(2,1)} %bitcast.66, bf16[]{:T(256)} %broadcast.94), dimensions={1}, to_apply=%bitcast.55.reduce_sub_computation | reduce | bytes 4194306
  75.4 2.0 reshape.136
  77.4 9.4 %all-to-all-start = ((bf16[16,2,32768]{2,1,0:T(2,128)(2,1)}), bf16[16,2,32768]{2,1,0:T(2,128)(2,1)}, u32[]{:S(2)}, u32[]{:S(2)}) async-start(bf16[16,2,32768]{2,1,0:T(2,128)(2,1)} %reshape.136), calls=%async_computation | async-start | bytes 4194304 | tf_op jit(solution)/shard_map/all_to_all | solution.py:89
  90.1 3.0 %copy.50 = bf16[128,9216]{0,1:T(8,128)(2,1)S(1)} copy(bf16[128,9216]{1,0:T(8,128)(2,1)} %param.13) | data formatting | bytes 4718592 | tf_op args[0]
  95.7 38.7 %all-to-all-done = bf16[16,2,32768]{2,1,0:T(2,128)(2,1)} async-done(((bf16[16,2,32768]{2,1,0:T(2,128)(2,1)}), bf16[16,2,32768]{2,1,0:T(2,128)(2,1)}, u32[]{:S(2)}, u32[]{:S(2)}) %all-to-all-start) | async-done | bytes 2097184 | tf_op jit(solution)/shard_map/all_to_all | solution.py:89
  134.4 10.4 %reshape.137 = bf16[8192,1,128]{2,1,0:T(2,128)(2,1)} reshape(bf16[16,2,32768]{2,1,0:T(2,128)(2,1)} %all-to-all-done) | data formatting | bytes 4194304
  144.8 3.8 %copy.72 = bf16[1,128,8192]{1,2,0:T(8,128)(2,1)} copy(bf16[1,128,8192]{1,0,2:T(2,128)(2,1)} %bitcast.67) | data formatting | bytes 4194304
  148.6 3.9 %copy.56 = bf16[1,128,16,512]{3,1,2,0:T(8,128)(2,1)} copy(bf16[1,128,16,512]{1,3,2,0:T(8,128)(2,1)} %bitcast.68) | data formatting | bytes 4194304 | tf_op jit(solution)/shard_map/all_to_all | solution.py:89
  152.5 3.6 %gather_fusion.1 = bf16[16,128,512]{2,1,0:T(8,128)(2,1)} fusion(bf16[16,128,512]{2,1,0:T(8,128)(2,1)} %bitcast.69, s32[1024]{0:T(1024)S(1)} %pad_clamp_fusion), kind=kCustom, calls=%fused_computation.1 | custom fusion | bytes 4194368 | tf_op jit(solution)/shard_map/jit(_take)/gather | solution.py:90
  156.1 3.2 %broadcast_select_fusion = bf16[16,128,512]{2,1,0:T(8,128)(2,1)} fusion(bf16[16,128,512]{2,1,0:T(8,128)(2,1)} %gather_fusion.1, pred[16]{0:T(512)(128)(4,1)S(1)} %compare_and_fusion), kind=kLoop, calls=%fused_computation.32 | loop fusion | flops 1048576 | bytes 4194320 | tf_op jit(solution)/shard_map/jit(_take)/select_n | solution.py:90
  159.2 4.9 %all-to-all-start.1 = ((bf16[16,128,512]{2,1,0:T(8,128)(2,1)}), bf16[16,128,512]{2,1,0:T(8,128)(2,1)}, u32[]{:S(2)}, u32[]{:S(2)}) async-start(bf16[16,128,512]{2,1,0:T(8,128)(2,1)} %broadcast_select_fusion), calls=%async_computation.1 | async-start | bytes 4194304 | tf_op jit(solution)/shard_map/all_to_all | solution.py:91
  165.1 2.0 copy.74
  168.8 1.8 maximum_convert_fusion
  170.7 11.8 %multiply_convert_fusion.1 = bf16[128,9216]{0,1:T(8,128)(2,1)S(1)} fusion(f32[131,9216]{0,1:T(8,128)S(1)} %maximum_convert_fusion, f32[9216]{0:T(1024)S(1)} %bitcast.85, f32[9216]{0:T(1024)S(1)} %bitcast.86, f32[9216]{0:T(1024)S(1)} %bitcast.84, f32[9216]{0:T(1024)S(1)} %bitcast.83, f32[9216]{0:T(1024)S(1)} %copy-done.5), kind=kLoop, calls=%fused_computation.14 | loop fusion | flops 15335424 | bytes 21417984 | tf_op jit(solution)/shard_map/convert_element_type | solution.py:20
  183.9 6.0 %fusion.4 = f32[4,32,64,128]{3,2,1,0:T(8,128)} fusion(bf16[128,4,32,64]{0,3,2,1:T(8,128)(2,1)S(1)} %bitcast.70, f32[4,32,128]{2,1,0:T(8,128)S(1)} %bitcast.88, f32[4,32,128]{2,1,0:T(8,128)S(1)} %bitcast.89, f32[4,128,128]{2,1,0:T(8,128)S(1)} %fusion.24, pred[128,128]{1,0:T(8,128)(4,1)S(1)} %iota_compare_fusion), kind=kOutput, calls=%fused_computation.15 | convolution fusion | flops 281018368 | bytes 6701056 | tf_op jit(solution)/shard_map/gjts,sgjp->tgjp/dot_general | solution.py:42
  189.9 21.7 %all-to-all-done.1 = bf16[16,128,512]{2,1,0:T(8,128)(2,1)} async-done(((bf16[16,128,512]{2,1,0:T(8,128)(2,1)}), bf16[16,128,512]{2,1,0:T(8,128)(2,1)}, u32[]{:S(2)}, u32[]{:S(2)}) %all-to-all-start.1) | async-done | bytes 2097184 | tf_op jit(solution)/shard_map/all_to_all | solution.py:91
  213.4 2.4 copy.57
  215.8 4.7 %fusion.9 = bf16[128,4,32,64]{0,3,2,1:T(8,128)(2,1)} fusion(bf16[128,4,32,64]{0,3,2,1:T(8,128)(2,1)} %bitcast.73, bf16[128,4,128,1]{0,2,3,1:T(8,128)(2,1)S(1)} %bitcast.81, bf16[128,4,32,64]{0,3,2,1:T(8,128)(2,1)} %bitcast.71, f32[128,4,32]{0,2,1:T(8,128)S(1)} %bitcast.87, f32[4,32]{1,0:T(4,128)S(1)} %exp.45), kind=kOutput, calls=%fused_computation.21 | convolution fusion | flops 275775488 | bytes 6488576 | tf_op jit(solution)/shard_map/sgn,sgjp->ngjp/dot_general | solution.py:49
  220.5 4.1 %copy.63 = bf16[1,128,8192]{2,1,0:T(8,128)(2,1)} copy(bf16[1,128,8192]{1,2,0:T(8,128)(2,1)} %bitcast.76) | data formatting | bytes 4194304
  224.5 5.2 %fusion.7 = bf16[128,4,32,64]{0,3,2,1:T(8,128)(2,1)} fusion(bf16[128,4,32,64]{0,3,2,1:T(8,128)(2,1)S(1)} %bitcast.72, f32[4,32,64,128]{3,2,1,0:T(8,128)} %fusion.4, bf16[128,4,32,64]{0,3,2,1:T(8,128)(2,1)} %bitcast.74, bf16[128,4,128,1]{0,2,3,1:T(8,128)(2,1)S(1)} %bitcast.78, f32[128,4,32]{0,2,1:T(8,128)S(1)} %bitcast.82, f32[4,32]{1,0:T(4,128)S(1)} %mul.134), kind=kOutput, calls=%fused_computation.18 | convolution fusion | flops 274726912 | bytes 10682880 | tf_op jit(solution)/shard_map/tgn,ngjp->tgjp/dot_general | solution.py:57
  229.7 4.1 %copy.62 = bf16[128,8192]{1,0:T(8,128)(2,1)} copy(bf16[128,8192]{0,1:T(8,128)(2,1)} %bitcast.75) | data formatting | bytes 4194304
  (57 shorter events, 13.3 us)
Async XLA Ops:
  7.2 157.0 %all-gather.2.cloned.1.call-start = ((), (), s32[]{:S(2)}) async-start(), calls=%async_computation.2 | async-start | bytes 3760128 | tf_op jit(solution)/shard_map/all_gather | solution.py:87
  75.4 11.5 %copy-start = (s32[16]{0:T(128)S(1)}, s32[16]{0:T(128)}, u32[]{:S(2)}) copy-start(s32[16]{0:T(128)} %param.22) | copy-start | bytes 196
  75.4 12.1 %copy-start.8 = (s32[16]{0:T(128)S(1)}, s32[16]{0:T(128)}, u32[]{:S(2)}) copy-start(s32[16]{0:T(128)} %param.23) | copy-start | bytes 196
  75.4 14.1 %copy-start.9 = (s32[16]{0:T(128)S(1)}, s32[16]{0:T(128)}, u32[]{:S(2)}) copy-start(s32[16]{0:T(128)} %param.24) | copy-start | bytes 196
  77.4 16.4 %copy-start.10 = (f32[128]{0:T(128)S(1)}, f32[128]{0:T(128)}, u32[]{:S(2)}) copy-start(f32[128]{0:T(128)} %param.18) | copy-start | bytes 1540
  77.4 16.4 %copy-start.3 = (f32[128,128]{1,0:T(8,128)S(1)}, f32[128,128]{1,0:T(8,128)}, u32[]{:S(2)}) copy-start(f32[128,128]{1,0:T(8,128)} %param.14) | copy-start | bytes 196612
  77.4 16.5 %copy-start.6 = (f32[128]{0:T(128)S(1)}, f32[128]{0:T(128)}, u32[]{:S(2)}) copy-start(f32[128]{0:T(128)} %param.17) | copy-start | bytes 1540
  77.4 57.0 %all-to-all-start = ((bf16[16,2,32768]{2,1,0:T(2,128)(2,1)}), bf16[16,2,32768]{2,1,0:T(2,128)(2,1)}, u32[]{:S(2)}, u32[]{:S(2)}) async-start(bf16[16,2,32768]{2,1,0:T(2,128)(2,1)} %reshape.136), calls=%async_computation | async-start | bytes 4194304 | tf_op jit(solution)/shard_map/all_to_all | solution.py:89
  86.8 7.8 %copy-start.7 = (f32[128]{0:T(128)S(1)}, f32[128]{0:T(128)}, u32[]{:S(2)}) copy-start(f32[128]{0:T(128)} %param.19) | copy-start | bytes 1540
  86.9 8.7 %copy-start.4 = (f32[4,9216]{1,0:T(4,128)S(1)}, f32[4,9216]{1,0:T(4,128)}, u32[]{:S(2)}) copy-start(f32[4,9216]{1,0:T(4,128)} %param.15) | copy-start | bytes 442372
  159.2 52.4 %all-to-all-start.1 = ((bf16[16,128,512]{2,1,0:T(8,128)(2,1)}), bf16[16,128,512]{2,1,0:T(8,128)(2,1)}, u32[]{:S(2)}, u32[]{:S(2)}) async-start(bf16[16,128,512]{2,1,0:T(8,128)(2,1)} %broadcast_select_fusion), calls=%async_computation.1 | async-start | bytes 4194304 | tf_op jit(solution)/shard_map/all_to_all | solution.py:91
  168.8 1.8 copy-start.5
  182.6 1.3 copy-start.1
  215.8 8.7 %copy-start.2 = (bf16[128,8192]{0,1:T(8,128)(2,1)S(1)}, bf16[128,8192]{0,1:T(8,128)(2,1)}, u32[]{:S(2)}) copy-start(bf16[128,8192]{0,1:T(8,128)(2,1)} %copy-done.1) | copy-start | bytes 6291460
Sparse Core Ops, SparseCore 0:
  10.3 48.3 all-gather.1
where the time goes:
time: 242 us; the launch traced here: 241 us
  other arithmetic  67 us (28%)
  waiting for transfers between devices  60.5 us (25%)
  local copies, waits for them, and re-layouts  55.7 us (23%)
  between operations  19 us (8%)
  matrix products  16.1 us (7%)
  starting transfers between devices  14.4 us (6%)
  blocking collectives  7.91 us (3%)
    unnamed x1, other arithmetic  45.2 us
    unnamed x34, local copies, waits for them, and re-layouts  39.9 us
    all_to_all x1, waiting for transfers between devices, local(): lax.all_to_all(send_states, 'req', split_axis=2, concat_axis=0, tiled=True)  38.7 us
    all_to_all x1, waiting for transfers between devices, local(): lax.all_to_all(state_chosen, 'req', split_axis=0, concat_axis=2, tiled=True)  21.7 us
    convert_element_type x1, other arithmetic, convolve(): return jax.nn.silu(conv).astype(jnp.bfloat16)  11.8 us
    all_to_all x1, starting transfers between devices, local(): lax.all_to_all(send_states, 'req', split_axis=2, concat_axis=0, tiled=True)  9.43 us
    unnamed x1, blocking collectives  7.91 us
    dot_general x1, matrix products, local_part(): jnp.einsum('gjts,sgjp->tgjp', mixing, inputs, preferred_element_type=jnp....  5.99 us
  transfers between devices with their start and end apart: 3, of which 2 were waited for; matrix products, arithmetic and copies ran while one was open for 47% of the time, Pallas kernels for 0%

commit v1 on v0

--- a/solution.py
+++ b/solution.py
@@ -88,7 +88,12 @@
     tail = lax.dynamic_index_in_dim(every_tail, own_row, 0, keepdims=False)
     state_parts = lax.all_to_all(send_states, "req", split_axis=2, concat_axis=0, tiled=True)
     state_chosen = jnp.take(state_parts, wanted_rows, axis=0)
-    start = lax.all_to_all(state_chosen, "req", split_axis=0, concat_axis=2, tiled=True)[0]
+    start = jnp.concatenate(
+        lax.all_to_all(
+            jnp.stack(jnp.split(state_chosen, lax.axis_size("req"), axis=0)), "req", 0, 0
+        ),
+        axis=2,
+    )[0]
     tail = jnp.where(live, tail, jnp.zeros_like(tail))
     start = jnp.where(live, start, jnp.zeros_like(start))
     conv_out = convolve(xbc, tail, conv_weight, conv_bias)

time: 242 us -> 272 us (1.12)
  waiting for transfers between devices: 60.5 us -> 81.3 us
  local copies, waits for them, and re-layouts: 55.7 us -> 66.6 us
    all_to_all x1, waiting for transfers between devices: 38.7 us -> 58.9 us  [local(): lax.all_to_all(send_states, 'req', split_axis=2, concat_axis=0, tiled=True)]
    unnamed x34 -> x49, local copies, waits for them, and re-layouts: 39.9 us -> 50.1 us
  transfers between devices with their start and end apart: 3 -> 3, of which waited for: 2 -> 2; matrix products, arithmetic and copies ran while one was open for 47% -> 24% of each run, Pallas kernels for 0% -> 0%
where the time goes in v1:
time: 272 us; the launch traced here: 271 us
  waiting for transfers between devices  81.3 us (30%)
  local copies, waits for them, and re-layouts  66.6 us (24%)
  other arithmetic  65.7 us (24%)
  between operations  18.9 us (7%)
  matrix products  15.9 us (6%)
  starting transfers between devices  14.2 us (5%)
  blocking collectives  7.88 us (3%)
    all_to_all x1, waiting for transfers between devices, local(): lax.all_to_all(send_states, 'req', split_axis=2, concat_axis=0, tiled=True)  58.9 us
    unnamed x49, local copies, waits for them, and re-layouts  50.1 us
    unnamed x1, other arithmetic  45.2 us
    all_to_all x1, waiting for transfers between devices, local(): lax.all_to_all(jnp.stack(jnp.split(state_chosen, lax.axis_size('req'), ax...  21.7 us
    convert_element_type x1, other arithmetic, convolve(): return jax.nn.silu(conv).astype(jnp.bfloat16)  11.8 us
    all_to_all x1, starting transfers between devices, local(): lax.all_to_all(send_states, 'req', split_axis=2, concat_axis=0, tiled=True)  9.43 us
    unnamed x1, blocking collectives  7.88 us
    dot_general x1, matrix products, local_part(): jnp.einsum('gjts,sgjp->tgjp', mixing, inputs, preferred_element_type=jnp....  5.99 us
  transfers between devices with their start and end apart: 3, of which 2 were waited for; matrix products, arithmetic and copies ran while one was open for 24% of the time, Pallas kernels for 0%

profile of v1, /device:TPU:15, one launch (start us, length us, event | category | flops | bytes accessed | tf_op | source)
XLA Modules:
  0.0 270.5 jit_solution(9919999493708812133)
XLA Ops:
  9.8 7.9 %all-reduce = s32[16]{0:T(128)S(1)} all-reduce(s32[16]{0:T(128)S(1)} %dynamic-update-slice), channel_id=1, replica_groups=mesh['grp'=2,'req'=16] {'req'}, use_global_device_ids=true, to_apply=%add | all-reduce | flops 16 | bytes 128
  20.9 1.7 constant_dynamic-slice_fusion
  22.7 6.9 %copy.88 = bf16[1,128,8192]{1,0,2:T(2,128)(2,1)} copy(bf16[1,128,8192]{2,1,0:T(8,128)(2,1)S(1)} %constant_dynamic-slice_fusion) | data formatting | bytes 4194304
  30.1 45.2 %reduce.4 = bf16[8192,128]{1,0:T(8,128)(2,1)S(1)} reduce(bf16[8192,1,128]{2,1,0:T(2,128)(2,1)} %bitcast.128, bf16[]{:T(256)} %broadcast.90), dimensions={1}, to_apply=%bitcast.117.reduce_sub_computation | reduce | bytes 4194306
  75.3 2.0 reshape.133
  77.3 9.4 %all-to-all-start = ((bf16[16,2,32768]{2,1,0:T(2,128)(2,1)}), bf16[16,2,32768]{2,1,0:T(2,128)(2,1)}, u32[]{:S(2)}, u32[]{:S(2)}) async-start(bf16[16,2,32768]{2,1,0:T(2,128)(2,1)} %reshape.133), calls=%async_computation | async-start | bytes 4194304 | tf_op jit(solution)/shard_map/all_to_all | solution.py:89
  88.7 3.1 %copy.65 = bf16[128,9216]{0,1:T(8,128)(2,1)S(1)} copy(bf16[128,9216]{1,0:T(8,128)(2,1)} %param.13) | data formatting | bytes 4718592 | tf_op args[0]
  96.3 58.9 %all-to-all-done = bf16[16,2,32768]{2,1,0:T(2,128)(2,1)} async-done(((bf16[16,2,32768]{2,1,0:T(2,128)(2,1)}), bf16[16,2,32768]{2,1,0:T(2,128)(2,1)}, u32[]{:S(2)}, u32[]{:S(2)}) %all-to-all-start) | async-done | bytes 2097184 | tf_op jit(solution)/shard_map/all_to_all | solution.py:89
  155.2 10.4 %reshape.134 = bf16[8192,1,128]{2,1,0:T(2,128)(2,1)} reshape(bf16[16,2,32768]{2,1,0:T(2,128)(2,1)} %all-to-all-done) | data formatting | bytes 4194304
  165.6 3.8 %copy.87 = bf16[1,128,8192]{1,2,0:T(8,128)(2,1)} copy(bf16[1,128,8192]{1,0,2:T(2,128)(2,1)} %bitcast.129) | data formatting | bytes 4194304
  169.4 3.9 %copy.71 = bf16[1,128,16,512]{3,1,2,0:T(8,128)(2,1)} copy(bf16[1,128,16,512]{1,3,2,0:T(8,128)(2,1)} %bitcast.130) | data formatting | bytes 4194304 | tf_op jit(solution)/shard_map/all_to_all | solution.py:89
  173.3 3.6 %gather_fusion.1 = bf16[16,128,512]{2,1,0:T(8,128)(2,1)} fusion(bf16[16,128,512]{2,1,0:T(8,128)(2,1)} %bitcast.131, s32[1024]{0:T(1024)S(1)} %pad_clamp_fusion), kind=kCustom, calls=%fused_computation.1 | custom fusion | bytes 4194368 | tf_op jit(solution)/shard_map/jit(_take)/gather | solution.py:90
  176.9 1.9 broadcast_select_fusion
  189.4 4.7 %all-to-all-start.1 = ((bf16[16,1,128,512]{3,2,1,0:T(8,128)(2,1)}), bf16[16,1,128,512]{3,2,1,0:T(8,128)(2,1)}, u32[]{:S(2)}, u32[]{:S(2)}) async-start(bf16[16,1,128,512]{3,2,1,0:T(8,128)(2,1)} %fusion.18), calls=%async_computation.1 | async-start | bytes 4194304 | tf_op jit(solution)/shard_map/all_to_all | solution.py:92
  195.0 2.0 copy.89
  198.8 1.8 maximum_convert_fusion
  200.6 11.8 %multiply_convert_fusion.1 = bf16[128,9216]{0,1:T(8,128)(2,1)S(1)} fusion(f32[131,9216]{0,1:T(8,128)S(1)} %maximum_convert_fusion, f32[9216]{0:T(1024)S(1)} %bitcast.147, f32[9216]{0:T(1024)S(1)} %bitcast.148, f32[9216]{0:T(1024)S(1)} %bitcast.146, f32[9216]{0:T(1024)S(1)} %bitcast.145, f32[9216]{0:T(1024)S(1)} %copy-done.5), kind=kLoop, calls=%fused_computation.14 | loop fusion | flops 15335424 | bytes 21417984 | tf_op jit(solution)/shard_map/convert_element_type | solution.py:20
  213.9 6.0 %fusion.4 = f32[4,32,64,128]{3,2,1,0:T(8,128)} fusion(bf16[128,4,32,64]{0,3,2,1:T(8,128)(2,1)S(1)} %bitcast.132, f32[4,32,128]{2,1,0:T(8,128)S(1)} %bitcast.150, f32[4,32,128]{2,1,0:T(8,128)S(1)} %bitcast.151, f32[4,128,128]{2,1,0:T(8,128)S(1)} %fusion.40, pred[128,128]{1,0:T(8,128)(4,1)S(1)} %iota_compare_fusion), kind=kOutput, calls=%fused_computation.15 | convolution fusion | flops 281018368 | bytes 6701056 | tf_op jit(solution)/shard_map/gjts,sgjp->tgjp/dot_general | solution.py:42
  219.9 21.7 %all-to-all-done.1 = bf16[16,1,128,512]{3,2,1,0:T(8,128)(2,1)} async-done(((bf16[16,1,128,512]{3,2,1,0:T(8,128)(2,1)}), bf16[16,1,128,512]{3,2,1,0:T(8,128)(2,1)}, u32[]{:S(2)}, u32[]{:S(2)}) %all-to-all-start.1) | async-done | bytes 2097184 | tf_op jit(solution)/shard_map/all_to_all | solution.py:92
  243.3 2.4 copy.72
  245.7 5.8 %fusion.7 = bf16[128,4,32,64]{0,3,2,1:T(8,128)(2,1)} fusion(bf16[128,4,32,64]{0,3,2,1:T(8,128)(2,1)} %bitcast.133, f32[4,32,64,128]{3,2,1,0:T(8,128)} %fusion.4, bf16[128,4,32,64]{0,3,2,1:T(8,128)(2,1)} %bitcast.135, bf16[128,4,128,1]{0,2,3,1:T(8,128)(2,1)S(1)} %bitcast.140, f32[128,4,32]{0,2,1:T(8,128)S(1)} %bitcast.144, f32[4,32]{1,0:T(4,128)S(1)} %mul.134), kind=kOutput, calls=%fused_computation.18 | convolution fusion | flops 274726912 | bytes 10682880 | tf_op jit(solution)/shard_map/tgn,ngjp->tgjp/dot_general | solution.py:57
  251.5 4.2 %copy.77 = bf16[128,8192]{1,0:T(8,128)(2,1)} copy(bf16[128,8192]{0,1:T(8,128)(2,1)} %bitcast.137) | data formatting | bytes 4194304
  255.7 3.9 %fusion.9 = bf16[128,4,32,64]{0,3,2,1:T(8,128)(2,1)} fusion(bf16[128,4,32,64]{0,3,2,1:T(8,128)(2,1)} %bitcast.136, bf16[128,4,128,1]{0,2,3,1:T(8,128)(2,1)S(1)} %bitcast.143, bf16[128,4,32,64]{0,3,2,1:T(8,128)(2,1)S(1)} %bitcast.134, f32[128,4,32]{0,2,1:T(8,128)S(1)} %bitcast.149, f32[4,32]{1,0:T(4,128)S(1)} %exp.45), kind=kOutput, calls=%fused_computation.21 | convolution fusion | flops 275775488 | bytes 6488576 | tf_op jit(solution)/shard_map/sgn,sgjp->ngjp/dot_general | solution.py:49
  259.6 4.1 %copy.78 = bf16[1,128,8192]{2,1,0:T(8,128)(2,1)} copy(bf16[1,128,8192]{1,2,0:T(8,128)(2,1)} %bitcast.138) | data formatting | bytes 4194304
  (73 shorter events, 24.6 us)
Async XLA Ops:
  77.3 10.2 %copy-start = (s32[16]{0:T(128)S(1)}, s32[16]{0:T(128)}, u32[]{:S(2)}) copy-start(s32[16]{0:T(128)} %param.22) | copy-start | bytes 196
  77.3 10.8 %copy-start.8 = (s32[16]{0:T(128)S(1)}, s32[16]{0:T(128)}, u32[]{:S(2)}) copy-start(s32[16]{0:T(128)} %param.23) | copy-start | bytes 196
  77.3 78.0 %all-to-all-start = ((bf16[16,2,32768]{2,1,0:T(2,128)(2,1)}), bf16[16,2,32768]{2,1,0:T(2,128)(2,1)}, u32[]{:S(2)}, u32[]{:S(2)}) async-start(bf16[16,2,32768]{2,1,0:T(2,128)(2,1)} %reshape.133), calls=%async_computation | async-start | bytes 4194304 | tf_op jit(solution)/shard_map/all_to_all | solution.py:89
  86.7 107.4 %all-gather.2.cloned.1.call-start = ((), (), s32[]{:S(2)}) async-start(), calls=%async_computation.2 | async-start | bytes 3760128 | tf_op jit(solution)/shard_map/all_gather | solution.py:87
  88.7 4.5 %copy-start.9 = (s32[16]{0:T(128)S(1)}, s32[16]{0:T(128)}, u32[]{:S(2)}) copy-start(s32[16]{0:T(128)} %param.24) | copy-start | bytes 196
  88.7 5.2 %copy-start.10 = (f32[128]{0:T(128)S(1)}, f32[128]{0:T(128)}, u32[]{:S(2)}) copy-start(f32[128]{0:T(128)} %param.18) | copy-start | bytes 1540
  88.7 5.2 %copy-start.3 = (f32[128,128]{1,0:T(8,128)S(1)}, f32[128,128]{1,0:T(8,128)}, u32[]{:S(2)}) copy-start(f32[128,128]{1,0:T(8,128)} %param.14) | copy-start | bytes 196612
  88.7 5.2 %copy-start.6 = (f32[128]{0:T(128)S(1)}, f32[128]{0:T(128)}, u32[]{:S(2)}) copy-start(f32[128]{0:T(128)} %param.17) | copy-start | bytes 1540
  88.7 5.4 %copy-start.4 = (f32[4,9216]{1,0:T(4,128)S(1)}, f32[4,9216]{1,0:T(4,128)}, u32[]{:S(2)}) copy-start(f32[4,9216]{1,0:T(4,128)} %param.15) | copy-start | bytes 442372
  88.7 6.6 %copy-start.7 = (f32[128]{0:T(128)S(1)}, f32[128]{0:T(128)}, u32[]{:S(2)}) copy-start(f32[128]{0:T(128)} %param.19) | copy-start | bytes 1540
  189.4 52.2 %all-to-all-start.1 = ((bf16[16,1,128,512]{3,2,1,0:T(8,128)(2,1)}), bf16[16,1,128,512]{3,2,1,0:T(8,128)(2,1)}, u32[]{:S(2)}, u32[]{:S(2)}) async-start(bf16[16,1,128,512]{3,2,1,0:T(8,128)(2,1)} %fusion.18), calls=%async_computation.1 | async-start | bytes 4194304 | tf_op jit(solution)/shard_map/all_to_all | solution.py:92
  198.8 1.8 copy-start.5
  212.5 1.3 copy-start.1
  251.5 4.2 %copy-start.2 = (bf16[128,8192]{0,1:T(8,128)(2,1)S(1)}, bf16[128,8192]{0,1:T(8,128)(2,1)}, u32[]{:S(2)}) copy-start(bf16[128,8192]{0,1:T(8,128)(2,1)} %copy-done.1) | copy-start | bytes 6291460
Sparse Core Ops, SparseCore 0:
  89.8 66.8 all-gather.1
